TPU v7x, 32 devices: a whole 2x2x4 slice. The times are simulated.
32 devices in a mesh: groups: 2 (over y), row: 4 (over z), col: 4 (over x, core).
Axes of the slice: x: 2, y: 2, z: 4, core: 2. Of those that a mesh axis runs over, the one named last changes fastest.
Arguments:
- pair_state: bfloat16 [160, 80, 128], P(('groups', 'row'), 'col'), parts along dimension 0, may hold values from -6 to 6
- token_mask: int32 [160], P('groups'), parts along dimension 0, may hold values 0 or 1
- norm_gain: float32 [128], replicated, may hold values from 0.1 to 1.9
- norm_bias: float32 [128], replicated, may hold values from -3 to 3
- proj_weight: bfloat16 [128, 512], replicated, may hold values from -0.5 to 0.5
- gate_weight: bfloat16 [128, 128], replicated, may hold values from -0.5 to 0.5
- tri_gain: float32 [128], replicated, may hold values from 0.1 to 1.9
- tri_bias: float32 [128], replicated, may hold values from -3 to 3
- out_weight: bfloat16 [128, 128], replicated, may hold values from -0.5 to 0.5
- trans_gain: float32 [128], replicated, may hold values from 0.1 to 1.9
- trans_bias: float32 [128], replicated, may hold values from -3 to 3
- trans_in: bfloat16 [128, 1024], replicated, may hold values from -0.5 to 0.5
- trans_out: bfloat16 [512, 128], replicated, may hold values from -0.25 to 0.25
Outputs:
- pair_columns: bfloat16 [160, 4, 20, 128], P('groups', 'col', 'row'), parts along dimension 0
There are 2 independent parts, one for each index of `groups`. A program takes and returns all parts, laid end to end along the dimension named above; an argument that names none is the same for every part. Nothing has to cross between parts.
All inputs are finite; a program needn't handle non-finite values.
Results may differ from a plain program's by a relative error of at most 0.0062.
Values may be sent and summed in bfloat16 or wider, within the bound.
A program may use at most 128 MiB of HBM per device.

v0:
```python
import jax
import jax.numpy as jnp
from jax import lax
from jax.sharding import PartitionSpec as P

epsilon = 1e-05


def layer_norm(values, gain, bias):
    center = jnp.mean(values, axis=-1, keepdims=True)
    spread = jnp.mean(jnp.square(values - center), axis=-1, keepdims=True)
    return (values - center) * lax.rsqrt(spread + epsilon) * gain + bias


def body(
    pair_state,
    token_mask,
    norm_gain,
    norm_bias,
    proj_weight,
    gate_weight,
    tri_gain,
    tri_bias,
    out_weight,
    trans_gain,
    trans_bias,
    trans_in,
    trans_out,
):
    rows_here, cols_here, channels = pair_state.shape
    hidden = proj_weight.shape[1] // 4
    expansion = trans_out.shape[0]
    row_index = lax.axis_index("row")
    col_index = lax.axis_index("col")
    weights = token_mask.astype(jnp.float32)
    row_weight = lax.dynamic_slice_in_dim(weights, row_index * rows_here, rows_here)
    col_weight = lax.dynamic_slice_in_dim(weights, col_index * cols_here, cols_here)
    normed = layer_norm(pair_state.astype(jnp.float32), norm_gain, norm_bias).astype(jnp.bfloat16)
    flattened = normed.reshape(-1, channels)
    projected = jnp.dot(flattened, proj_weight, preferred_element_type=jnp.float32)
    projected = projected.reshape(rows_here, cols_here, 4 * hidden)
    pair_weight = (row_weight[:, None] * col_weight[None, :])[:, :, None]
    left_panel = (
        pair_weight * jax.nn.sigmoid(projected[..., hidden : 2 * hidden]) * projected[..., :hidden]
    ).astype(jnp.bfloat16)
    right_panel = (
        pair_weight
        * jax.nn.sigmoid(projected[..., 3 * hidden :])
        * projected[..., 2 * hidden : 3 * hidden]
    ).astype(jnp.bfloat16)
    right_all = lax.all_gather(right_panel, "row", axis=0, tiled=True)
    summed = lax.psum_scatter(
        jnp.einsum("jkc,ikc->jic", right_all, left_panel, preferred_element_type=jnp.float32),
        "col",
        scatter_dimension=0,
        tiled=True,
    )
    triangle = jnp.transpose(summed, (1, 0, 2))
    tri_normed = layer_norm(triangle, tri_gain, tri_bias).astype(jnp.bfloat16)
    branch = jnp.dot(tri_normed.reshape(-1, hidden), out_weight, preferred_element_type=jnp.float32)
    gate_value = jax.nn.sigmoid(jnp.dot(flattened, gate_weight, preferred_element_type=jnp.float32))
    updated = (pair_state.reshape(-1, channels).astype(jnp.float32) + gate_value * branch).astype(
        jnp.bfloat16
    )
    row_count_axis = lax.axis_size("row")
    sectioned = updated.reshape(rows_here, row_count_axis, cols_here // row_count_axis, channels)
    item_block = lax.all_to_all(sectioned, "row", split_axis=1, concat_axis=0, tiled=True)
    trans_normed = layer_norm(item_block.astype(jnp.float32), trans_gain, trans_bias).astype(
        jnp.bfloat16
    )
    hidden_act = jnp.dot(
        trans_normed.reshape(-1, channels), trans_in, preferred_element_type=jnp.float32
    )
    activated = (jax.nn.silu(hidden_act[:, :expansion]) * hidden_act[:, expansion:]).astype(
        jnp.bfloat16
    )
    result = item_block.reshape(-1, channels).astype(jnp.float32) + jnp.dot(
        activated, trans_out, preferred_element_type=jnp.float32
    )
    return result.astype(jnp.bfloat16).reshape(item_block.shape)


def solution(mesh):
    in_specs = (
        P(("groups", "row"), "col", None),
        P("groups"),
        P(),
        P(),
        P(),
        P(),
        P(),
        P(),
        P(),
        P(),
        P(),
        P(),
        P(),
    )
    out_specs = P("groups", "col", "row", None)
    return jax.shard_map(body, mesh=mesh, in_specs=in_specs, out_specs=out_specs, check_vma=False)
```

profile of v0, /device:TPU:0, one launch (start us, length us, event | category | flops | bytes accessed | tf_op | source)
XLA Modules:
  0.0 90.8 jit_solution(1624541455551044872)
XLA Ops:
  6.5 0.0 copy-start
  6.5 0.0 reduce-scatter.2.cloned.1.call-start
  6.5 0.7 convert_element_type.67
  7.2 1.0 %convert_reduce_fusion = f32[20,20]{1,0:T(8,128)S(1)} fusion(bf16[20,20,128]{2,1,0:T(8,128)(2,1)} %param.13), kind=kLoop, calls=%fused_computation.35 | loop fusion | flops 102000 | bytes 104000 | tf_op jit(solution)/shard_map/reduce_sum | solution.py:10
  8.3 1.1 %multiply_reduce_fusion.2 = f32[20,20]{1,0:T(8,128)S(1)} fusion(bf16[20,20,128]{2,1,0:T(8,128)(2,1)} %param.13, f32[20,20]{1,0:T(8,128)S(1)} %broadcast_multiply_fusion.3), kind=kLoop, calls=%fused_computation.33 | loop fusion | flops 204400 | bytes 105600 | tf_op jit(solution)/shard_map/reduce_sum | solution.py:11
  9.5 0.1 fusion.27
  9.5 0.1 broadcast_multiply_fusion.1
  9.6 1.1 %add_convert_fusion.1 = bf16[20,20,128]{2,1,0:T(8,128)(2,1)S(1)} fusion(bf16[20,20,128]{2,1,0:T(8,128)(2,1)} %param.13, f32[128]{0:T(128)} %param.16, f32[128]{0:T(128)} %param.15, f32[20,20]{1,0:T(8,128)S(1)} %add_rsqrt_fusion.2, f32[20,20]{1,0:T(8,128)S(1)} %broadcast_multiply_fusion.3), kind=kLoop, calls=%fused_computation.32 | loop fusion | flops 307200 | bytes 209024 | tf_op jit(solution)/shard_map/convert_element_type | solution.py:38
  10.7 1.2 %fusion.18 = f32[20,20,512]{2,1,0:T(8,128)S(1)} fusion(bf16[20,20,128]{2,1,0:T(8,128)(2,1)S(1)} %add_convert_fusion.1, bf16[128,512]{1,0:T(8,128)(2,1)} %param.17), kind=kOutput, calls=%fused_computation.36 | convolution fusion | flops 52428800 | bytes 1052672 | tf_op jit(solution)/shard_map/dot_general | solution.py:40
  11.9 0.8 fusion.8
  12.7 17.0 %all_gather.3 = bf16[80,20,128]{2,1,0:T(8,128)(2,1)S(1)} all-gather(bf16[20,20,128]{2,1,0:T(8,128)(2,1)S(1)} %get-tuple-element.5), channel_id=1, replica_groups=mesh['groups'=2,'row'=4,'col'=4] {'row'}, dimensions={0}, use_global_device_ids=true | all-gather | bytes 512000 | tf_op jit(solution)/shard_map/all_gather | solution.py:51
  29.7 1.5 %copy.69 = bf16[80,20,128]{1,0,2:T(8,128)(2,1)S(1)} copy(bf16[80,20,128]{2,1,0:T(8,128)(2,1)S(1)} %all_gather.3) | data formatting | bytes 819200 | tf_op jit(solution)/shard_map/all_gather | solution.py:51
  31.2 2.2 %copy.68 = bf16[20,20,128]{1,0,2:T(8,128)(2,1)} copy(bf16[20,20,128]{2,1,0:T(8,128)(2,1)} %get-tuple-element.6) | data formatting | bytes 204800 | tf_op jit(solution)/shard_map/convert_element_type | solution.py:45
  33.4 3.8 %convolution_bitcast_fusion = f32[80,20,128]{0,1,2:T(8,128)} fusion(bf16[20,20,128]{1,0,2:T(8,128)(2,1)} %copy.68, bf16[80,20,128]{1,0,2:T(8,128)(2,1)S(1)} %copy.69), kind=kOutput, calls=%fused_computation | convolution fusion | flops 8192000 | bytes 1331200 | tf_op jit(solution)/shard_map/jkc,ikc->jic/dot_general | solution.py:53
  37.2 0.0 copy-start.1
  37.2 0.0 copy-start.8
  37.2 2.8 %copy.70 = f32[80,20,128]{2,1,0:T(8,128)} copy(f32[80,20,128]{0,1,2:T(8,128)} %convolution_bitcast_fusion) | data formatting | bytes 1638400 | tf_op jit(solution)/shard_map/jkc,ikc->jic/transpose | solution.py:53
  40.0 0.0 copy-start.3
  40.0 0.0 copy-start.4
  40.0 0.0 reduce-scatter.2.cloned.1.call-update
  40.0 0.0 copy-start.2
  40.1 0.0 copy-done.1
  40.1 0.0 copy-done.8
  40.1 0.2 fusion.3
  40.3 26.2 %reduce-scatter.2.cloned.1.call-done = f32[20,20,128]{2,1,0:T(8,128)} async-done(((f32[80,20,128]{2,1,0:T(8,128)}), f32[20,20,128]{2,1,0:T(8,128)}) %reduce-scatter.2.cloned.1.call-update) | async-done | bytes 204816 | tf_op jit(solution)/shard_map/reduce_scatter | solution.py:52
  66.5 1.1 %bitcast_reduce_fusion = f32[20,20]{0,1:T(8,128)S(1)} fusion(f32[20,20,128]{2,1,0:T(8,128)} %reduce-scatter.2.cloned.1.call-done), kind=kLoop, calls=%fused_computation.28 | loop fusion | flops 50800 | bytes 206400 | tf_op jit(solution)/shard_map/reduce_sum | solution.py:10
  67.6 0.1 copy.71
  67.7 0.1 copy.72
  67.8 1.2 %multiply_reduce_fusion.1 = f32[20,20]{0,1:T(8,128)S(1)} fusion(f32[20,20,128]{2,1,0:T(8,128)} %reduce-scatter.2.cloned.1.call-done, f32[20,20]{0,1:T(8,128)S(1)} %copy.72), kind=kLoop, calls=%fused_computation.31 | loop fusion | flops 153200 | bytes 208000 | tf_op jit(solution)/shard_map/reduce_sum | solution.py:11
  69.0 0.1 copy.73
  69.1 0.1 copy.74
  69.2 0.0 copy-done.3
  69.2 0.0 copy-done.4
  69.2 1.1 %add_convert_fusion = bf16[20,20,128]{2,0,1:T(8,128)(2,1)S(1)} fusion(f32[20,20,128]{2,1,0:T(8,128)} %reduce-scatter.2.cloned.1.call-done, f32[128]{0:T(128)S(1)} %copy-done.3, f32[128]{0:T(128)S(1)} %copy-done.4, f32[20,20]{0,1:T(8,128)S(1)} %copy.74, f32[20,20]{0,1:T(8,128)S(1)} %copy.72), kind=kLoop, calls=%fused_computation.30 | loop fusion | flops 256000 | bytes 311424 | tf_op jit(solution)/shard_map/convert_element_type | solution.py:59
  70.4 0.0 copy-done.2
  70.4 0.0 copy-start.5
  70.4 0.0 copy-start.6
  70.5 0.2 fusion.5
  70.8 10.4 %all_to_all.4 = bf16[20,4,5,128]{3,0,2,1:T(8,128)(2,1)S(1)} all-to-all(bf16[20,4,5,128]{3,0,2,1:T(8,128)(2,1)S(1)} %copy.76), channel_id=1, replica_groups=mesh['groups'=2,'row'=4,'col'=4] {'row'}, dimensions={1} | all-to-all | bytes 204800 | tf_op jit(solution)/shard_map/all_to_all | solution.py:67
  81.2 0.1 fusion.20
  81.3 0.1 copy.80
  81.4 0.2 multiply_reduce_fusion
  81.7 0.1 copy.84
  81.8 0.2 rsqrt.30
  82.0 0.0 copy-start.7
  82.0 0.1 copy.77
  82.1 0.2 div.41
  82.3 0.0 copy-done
  82.3 0.0 copy-done.5
  82.3 0.0 copy-done.6
  82.3 0.4 fusion.21
  82.7 0.2 copy-done.7
  82.9 0.4 fusion.4
  83.3 0.7 copy.85
  (15 shorter events, 0.3 us)
Async XLA Ops:
  6.5 75.7 %copy-start = (bf16[128,1024]{1,0:T(8,128)(2,1)S(1)}, bf16[128,1024]{1,0:T(8,128)(2,1)}, u32[]{:S(2)}) copy-start(bf16[128,1024]{1,0:T(8,128)(2,1)} %param.24) | copy-start | bytes 786436
  6.5 60.0 %reduce-scatter.2.cloned.1.call-start = ((), (), s32[]{:S(2)}) async-start(), calls=%async_computation.2 | async-start | bytes 1228800 | tf_op jit(solution)/shard_map/reduce_scatter | solution.py:52
  37.2 2.9 %copy-start.1 = (bf16[20,20,128]{2,1,0:T(8,128)(2,1)S(1)}, bf16[20,20,128]{2,1,0:T(8,128)(2,1)}, u32[]{:S(2)}) copy-start(bf16[20,20,128]{2,1,0:T(8,128)(2,1)} %param.13) | copy-start | bytes 307204
  37.2 3.0 %copy-start.8 = (bf16[128,128]{1,0:T(8,128)(2,1)S(1)}, bf16[128,128]{1,0:T(8,128)(2,1)}, u32[]{:S(2)}) copy-start(bf16[128,128]{1,0:T(8,128)(2,1)} %param.18) | copy-start | bytes 98308
  40.0 29.2 %copy-start.3 = (f32[128]{0:T(128)S(1)}, f32[128]{0:T(128)}, u32[]{:S(2)}) copy-start(f32[128]{0:T(128)} %param.20) | copy-start | bytes 1540
  40.0 29.2 %copy-start.4 = (f32[128]{0:T(128)S(1)}, f32[128]{0:T(128)}, u32[]{:S(2)}) copy-start(f32[128]{0:T(128)} %param.19) | copy-start | bytes 1540
  40.0 30.4 %copy-start.2 = (bf16[128,128]{1,0:T(8,128)(2,1)S(1)}, bf16[128,128]{1,0:T(8,128)(2,1)}, u32[]{:S(2)}) copy-start(bf16[128,128]{1,0:T(8,128)(2,1)} %param.21) | copy-start | bytes 98308
  70.4 11.9 %copy-start.5 = (f32[128]{0:T(128)S(1)}, f32[128]{0:T(128)}, u32[]{:S(2)}) copy-start(f32[128]{0:T(128)} %param.23) | copy-start | bytes 1540
  70.4 11.9 %copy-start.6 = (f32[128]{0:T(128)S(1)}, f32[128]{0:T(128)}, u32[]{:S(2)}) copy-start(f32[128]{0:T(128)} %param.22) | copy-start | bytes 1540
  82.0 0.9 copy-start.7
Sparse Core Ops, SparseCore 0:
  40.1 26.3 reduce-scatter.1
where the time goes:
time: 91.3 us; the launch traced here: 90.8 us
  blocking collectives  27.4 us (30%)
  waiting for transfers between devices  26.2 us (29%)
  between operations  13.7 us (15%)
  other arithmetic  8.74 us (10%)
  local copies, waits for them, and re-layouts  8.7 us (10%)
  matrix products  6.16 us (7%)
    reduce_scatter x1, waiting for transfers between devices, body(): lax.psum_scatter(jnp.einsum('jkc,ikc->jic', right_all, left_panel, prefer...  26.2 us
    all_gather x1, blocking collectives, body(): right_all = lax.all_gather(right_panel, 'row', axis=0, tiled=True)  17 us
    all_to_all x1, blocking collectives, body(): lax.all_to_all(sectioned, 'row', split_axis=1, concat_axis=0, tiled=True)  10.4 us
    dot_general x1, matrix products, body(): jnp.einsum('jkc,ikc->jic', right_all, left_panel, preferred_element_type=...  3.78 us
    transpose x1, local copies, waits for them, and re-layouts, body(): jnp.einsum('jkc,ikc->jic', right_all, left_panel, preferred_element_type=...  2.83 us
    reduce_sum x3, other arithmetic, layer_norm(): spread = jnp.mean(jnp.square(values - center), axis=-1, keepdims=True)  2.59 us
    reduce_sum x3, other arithmetic, layer_norm(): center = jnp.mean(values, axis=-1, keepdims=True)  2.25 us
    convert_element_type x1, local copies, waits for them, and re-layouts, body(): left_panel = (pair_weight * jax.nn.sigmoid(projected[..., hidden:2 * hidd...  2.18 us
  transfers between devices with their start and end apart: 1, of which 1 were waited for; matrix products, arithmetic and copies ran while one was open for 0% of the time, Pallas kernels for 0%

commit v1 on v0

v1 whole, which is shorter than its diff:
```python
import functools

import jax
import jax.numpy as jnp
from jax import lax
from jax.experimental import pallas as pl
from jax.experimental.pallas import tpu as pltpu
from jax.sharding import PartitionSpec as P

epsilon = 1e-05
MESH = pl.DeviceIdType.MESH
f32 = jnp.float32
bf16 = jnp.bfloat16


def layer_norm(values, gain, bias):
    center = jnp.mean(values, axis=-1, keepdims=True)
    moved = values - center
    spread = jnp.mean(jnp.square(moved), axis=-1, keepdims=True)
    return moved * lax.rsqrt(spread + epsilon) * gain + bias


def sigmoid(values):
    return 0.5 * jnp.tanh(0.5 * values) + 0.5


def chunk_of(total):
    return max(size for size in range(16, 513, 16) if total % size == 0)


def nearest(me, step, count):
    ends = jnp.minimum(me, count - 1 - me)
    between = jnp.where(step % 2 == 1, me + (step + 1) // 2, me - step // 2)
    outside = jnp.where(me <= count - 1 - me, step, count - 1 - step)
    return jnp.where(step <= 2 * ends, between, outside)


def kernel(
    n_row, n_col,
    pair_ref, mask_ref, norm_gain, norm_bias, proj_ref, gate_ref, tri_gain, tri_bias, out_w_ref,
    trans_gain, trans_bias, trans_in, trans_out,
    out_ref,
    flat, work, left_t, right_f, gate, part, own, tri, msg, wide,
    right_all, sum_send, sum_recv, upd_send, upd_recv,
    a_send, a_recv, b_send, b_recv, c_send, c_recv,
):
    rows, cols, channels = pair_ref.shape
    hidden = proj_ref.shape[1] // 4
    tokens = mask_ref.shape[1]
    total = rows * cols
    piece = cols // n_row
    ratio = cols // rows
    expansion = trans_out.shape[0]
    chunk = chunk_of(total)
    r = lax.axis_index("row")
    q = lax.axis_index("col")

    barrier = pltpu.get_barrier_semaphore()
    for d in range(1, n_row):
        pl.semaphore_signal(barrier, inc=1, device_id={"row": lax.rem(r + d, n_row)}, device_id_type=MESH)
    for d in range(1, n_col):
        pl.semaphore_signal(barrier, inc=1, device_id={"col": lax.rem(q + d, n_col)}, device_id_type=MESH)

    def over_chunks(step):
        if chunk == total:
            step(0)
        else:
            pl.loop(0, total // chunk)(lambda n: step(pl.multiple_of(n * chunk, 16)))

    for i in range(rows):
        flat[i * cols:(i + 1) * cols, :] = pair_ref[i].astype(f32)

    def pair_weight(base):
        spot = lax.broadcasted_iota(jnp.int32, (chunk, tokens), 0).astype(f32) + (
            jnp.asarray(base, jnp.int32).astype(f32))
        token = lax.broadcasted_iota(jnp.int32, (chunk, tokens), 1).astype(f32)
        row_of = jnp.floor((spot + 0.5) * (1.0 / cols))
        col_of = spot - row_of * cols
        first = (token == row_of + (r * rows).astype(f32)).astype(f32)
        second = (token == col_of + (q * cols).astype(f32)).astype(f32)
        picked = ((first + second) * mask_ref[...].astype(f32)).astype(bf16)
        both = jnp.dot(picked, jnp.ones((tokens, hidden), bf16), preferred_element_type=f32)
        return (both > 1.5).astype(f32)

    def project(base):
        at = pl.ds(base, chunk)
        normed = layer_norm(flat[at, :], norm_gain[...], norm_bias[...]).astype(bf16)
        weight = pair_weight(base)
        right = jnp.dot(normed, proj_ref[:, 2 * hidden:], preferred_element_type=f32)
        panel = weight * sigmoid(right[:, hidden:]) * right[:, :hidden]
        right_all[r, at, :] = panel.astype(bf16)

    def project_left(base):
        at = pl.ds(base, chunk)
        normed = layer_norm(flat[at, :], norm_gain[...], norm_bias[...]).astype(bf16)
        weight = pair_weight(base)
        left = jnp.dot(normed, proj_ref[:, :2 * hidden], preferred_element_type=f32)
        panel = weight * sigmoid(left[:, hidden:]) * left[:, :hidden]
        work[at, :] = panel.astype(bf16).astype(f32)
        gate[at, :] = sigmoid(jnp.dot(normed, gate_ref[...], preferred_element_type=f32))

    over_chunks(project)
    pl.semaphore_wait(barrier, n_row - 1 + n_col - 1)

    def right_copy(block, slot, peer):
        return pltpu.make_async_remote_copy(
            src_ref=right_all.at[block], dst_ref=right_all.at[block],
            send_sem=a_send.at[slot], recv_sem=a_recv.at[block],
            device_id={"row": peer}, device_id_type=MESH)

    @pl.loop(1, n_row)
    def _(step):
        right_copy(r, step, nearest(r, step, n_row)).start()

    over_chunks(project_left)
    for k in range(cols):
        left_t[k] = work[pl.ds(k, rows, stride=cols), :]

    def sum_copy(block, peer):
        return pltpu.make_async_remote_copy(
            src_ref=sum_send.at[block], dst_ref=sum_recv.at[q, block % ratio],
            send_sem=b_send.at[block], recv_sem=b_recv.at[q, block % ratio],
            device_id={"col": peer}, device_id_type=MESH)

    span = chunk_k = next(size for size in (20, 16, 10, 8, 5, 4, 2, 1) if cols % size == 0)

    def triangle(block):
        right_f[...] = right_all[block].astype(f32)

        @pl.loop(0, rows // piece)
        def _(part_j):
            def steps(base_k, sums):
                sums = list(sums)
                for k in range(chunk_k):
                    mine = left_t[base_k * span + k]
                    for j in range(piece):
                        place = (part_j * piece + j) * cols + base_k * span + k
                        sums[j] = sums[j] + mine * right_f[pl.ds(place, 1), :]
                return tuple(sums)
            sums = tuple(jnp.zeros((rows, hidden), f32) for _ in range(piece))
            if chunk_k == cols:
                sums = steps(0, sums)
            else:
                sums = lax.fori_loop(0, cols // chunk_k, steps, sums)
            for j in range(piece):
                part[pl.ds(part_j * piece + j, rows, stride=rows), :] = sums[j]

        owner = block // ratio

        @pl.when(owner == q)
        def _():
            own[block % ratio] = part[...]

        @pl.when(owner != q)
        def _():
            sum_send[block] = part[...].astype(bf16)
            sum_copy(block, owner).start()

    triangle(r)

    @pl.loop(1, n_row)
    def _(step):
        block = nearest(r, step, n_row)
        right_copy(block, step, block).wait_recv()
        triangle(block)

    for half in range(ratio):
        sums = own[half]
        for d in range(1, n_col):
            other = lax.rem(q + d, n_col)
            pltpu.make_async_remote_copy(
                src_ref=sum_send.at[0], dst_ref=sum_recv.at[other, half],
                send_sem=b_send.at[0], recv_sem=b_recv.at[other, half],
                device_id={"col": other}, device_id_type=MESH).wait_recv()
            sums = sums + sum_recv[other, half].astype(f32)
        if ratio == 1:
            tri[...] = sums
        else:
            part[...] = sums
            for i in range(rows):
                tri[i * cols + half * rows:i * cols + (half + 1) * rows, :] = part[i * rows:(i + 1) * rows, :]

    def update(base):
        at = pl.ds(base, chunk)
        normed = layer_norm(tri[at, :], tri_gain[...], tri_bias[...]).astype(bf16)
        branch = jnp.dot(normed, out_w_ref[...], preferred_element_type=f32)
        work[at, :] = flat[at, :] + gate[at, :] * branch

    over_chunks(update)

    def upd_copy(slot, place, peer):
        return pltpu.make_async_remote_copy(
            src_ref=upd_send.at[slot], dst_ref=upd_recv.at[place],
            send_sem=c_send.at[slot], recv_sem=c_recv.at[place],
            device_id={"row": peer}, device_id_type=MESH)

    msg[...] = jnp.zeros_like(msg)

    @pl.loop(0, n_row)
    def _(step):
        target = nearest(r, n_row - 1 - step, n_row)
        for j in range(piece):
            msg[j * rows:(j + 1) * rows, :] = work[pl.ds(target * piece + j, rows, stride=cols), :]

        @pl.when(target == r)
        def _():
            upd_recv[r] = msg[...].astype(bf16)

        @pl.when(target != r)
        def _():
            upd_send[target] = msg[...].astype(bf16)
            upd_copy(target, r, target).start()

    def transition(source):
        state = upd_recv[source].astype(f32)
        normed = layer_norm(state, trans_gain[...], trans_bias[...]).astype(bf16)
        inner = jnp.dot(normed, trans_in[...], preferred_element_type=f32)
        swish = inner[:, :expansion]
        active = (swish * sigmoid(swish) * inner[:, expansion:]).astype(bf16)
        result = state + jnp.dot(active, trans_out[...], preferred_element_type=f32)
        for j in range(piece):
            wide[pl.ds(j, rows, stride=8), :] = result[j * rows:(j + 1) * rows, :]
        out_ref[pl.ds(source * rows, rows), 0] = wide[...].reshape(rows, 8, channels)[:, :piece].astype(bf16)

    wide[...] = jnp.zeros_like(wide)
    transition(r)

    @pl.loop(1, n_row)
    def _(step):
        source = nearest(r, step, n_row)
        upd_copy(source, source, source).wait_recv()
        transition(source)

    @pl.loop(1, n_row)
    def _(step):
        peer = nearest(r, step, n_row)
        right_copy(r, step, peer).wait_send()
        upd_copy(peer, r, peer).wait_send()

    @pl.loop(0, n_row)
    def _(block):
        @pl.when(block // ratio != q)
        def _():
            sum_copy(block, block // ratio).wait_send()


def body(n_row, n_col, pair_state, token_mask, norm_gain, norm_bias, proj_weight, gate_weight,
         tri_gain, tri_bias, out_weight, trans_gain, trans_bias, trans_in, trans_out):
    rows, cols, channels = pair_state.shape
    hidden = proj_weight.shape[1] // 4
    piece = cols // n_row
    ratio = cols // rows
    padded = -(-piece * rows // 16) * 16
    flat = lambda count: pltpu.VMEM((count, hidden), f32)
    line = lambda values: values.reshape(1, -1)
    return pl.pallas_call(
        functools.partial(kernel, n_row, n_col),
        out_shape=jax.ShapeDtypeStruct((rows * n_row, 1, piece, channels), bf16),
        in_specs=[pl.BlockSpec(memory_space=pltpu.VMEM)] * 13,
        out_specs=pl.BlockSpec(memory_space=pltpu.VMEM),
        scratch_shapes=[
            flat(rows * cols), flat(rows * cols),
            pltpu.VMEM((cols, rows, hidden), f32),
            flat(rows * cols), flat(rows * cols), flat(rows * rows),
            pltpu.VMEM((ratio, rows * rows, hidden), f32),
            flat(rows * cols), flat(padded), flat(rows * 8),
            pltpu.VMEM((n_row, rows * cols, hidden), bf16),
            pltpu.VMEM((n_row, rows * rows, hidden), bf16),
            pltpu.VMEM((n_col, ratio, rows * rows, hidden), bf16),
            pltpu.VMEM((n_row, padded, channels), bf16),
            pltpu.VMEM((n_row, padded, channels), bf16),
            pltpu.SemaphoreType.DMA((n_row,)), pltpu.SemaphoreType.DMA((n_row,)),
            pltpu.SemaphoreType.DMA((n_row,)), pltpu.SemaphoreType.DMA((n_col, ratio)),
            pltpu.SemaphoreType.DMA((n_row,)), pltpu.SemaphoreType.DMA((n_row,)),
        ],
        compiler_params=pltpu.CompilerParams(
            collective_id=0, has_side_effects=True, vmem_limit_bytes=56 * 1024 * 1024),
    )(pair_state, line(token_mask), line(norm_gain), line(norm_bias), proj_weight, gate_weight,
      line(tri_gain), line(tri_bias), out_weight, line(trans_gain), line(trans_bias), trans_in, trans_out)


def solution(mesh):
    in_specs = (P(("groups", "row"), "col", None), P("groups")) + (P(),) * 11
    out_specs = P("groups", "col", "row", None)
    return jax.shard_map(
        functools.partial(body, mesh.shape["row"], mesh.shape["col"]),
        mesh=mesh, in_specs=in_specs, out_specs=out_specs, check_vma=False)
```

time: 91.3 us -> 29.9 us (0.33)
  Pallas kernels: 0 us -> 28.2 us
  blocking collectives: 27.4 us -> 0 us
  waiting for transfers between devices: 26.2 us -> 0 us
  between operations: 13.7 us -> 0.01 us
  other arithmetic: 8.74 us -> 0 us
  local copies, waits for them, and re-layouts: 8.7 us -> 1.57 us
  matrix products: 6.16 us -> 0 us
    pallas_call x0 -> x1, Pallas kernels: none -> 28.2 us  [body(): pl.pallas_call(functools.partial(kernel, n_row, n_col), out_shape=jax.Sha...]
    reduce_scatter x1 -> x0, waiting for transfers between devices: 26.2 us -> none  [body(): lax.psum_scatter(jnp.einsum('jkc,ikc->jic', right_all, left_panel, prefer...]
    all_gather x1 -> x0, blocking collectives: 17 us -> none  [body(): right_all = lax.all_gather(right_panel, 'row', axis=0, tiled=True)]
    all_to_all x1 -> x0, blocking collectives: 10.4 us -> none  [body(): lax.all_to_all(sectioned, 'row', split_axis=1, concat_axis=0, tiled=True)]
    dot_general x6 -> x0, matrix products: 6.16 us -> none  [the longest x1 3.78 us: body(): jnp.einsum('jkc,ikc->jic', right_all, left_panel, preferred_element_type=...]
    reduce_sum x6 -> x0, other arithmetic: 4.84 us -> none  [the longest x3 2.59 us: layer_norm(): spread = jnp.mean(jnp.square(values - center), axis=-1, keepdims=True)]
    convert_element_type x5 -> x0, other arithmetic: 3.78 us -> none  [the longest x1 1.14 us: body(): tri_normed = layer_norm(triangle, tri_gain, tri_bias).astype(jnp.bfloat16)]
    transpose x1 -> x0, local copies, waits for them, and re-layouts: 2.83 us -> none  [body(): jnp.einsum('jkc,ikc->jic', right_all, left_panel, preferred_element_type=...]
  transfers between devices with their start and end apart: 1 -> 0, of which waited for: 1 -> 0; matrix products, arithmetic and copies ran while one was open for 0% -> 0% of each run, Pallas kernels for 0% -> 0%
where the time goes in v1:
time: 29.9 us; the launch traced here: 29.7 us
  Pallas kernels  28.2 us (94%)
  local copies, waits for them, and re-layouts  1.57 us (5%)
    pallas_call x1, Pallas kernels, body(): pl.pallas_call(functools.partial(kernel, n_row, n_col), out_shape=jax.Sha...  28.2 us
    pallas_call x1, local copies, waits for them, and re-layouts, body(): pl.pallas_call(functools.partial(kernel, n_row, n_col), out_shape=jax.Sha...  1.57 us

profile of v1, /device:TPU:0, one launch (start us, length us, event | category | flops | bytes accessed | tf_op | source)
XLA Modules:
  0.0 29.7 jit_solution(7237966112578284630)
XLA Ops:
  0.0 28.2 %shard_map.127 = bf16[80,1,5,128]{3,2,1,0:T(8,128)(2,1)} custom-call(bf16[20,20,128]{2,1,0:T(8,128)(2,1)} %pair_ref.1, s32[1,80]{1,0:T(1,128)} %bitcast.7, f32[1,128]{1,0:T(1,128)} %bitcast.8, f32[1,128]{1,0:T(1,128)} %bitcast.9, bf16[128,512]{1,0:T(8,128)(2,1)} %proj_ref.1, bf16[128,128]{1,0:T(8,128)(2,1)} %gate_ref.1, f32[1,128]{1,0:T(1,128)} %bitcast.10, ...), custom_call_target="tpu_custom_call" | custom-call | tf_op jit(solution)/shard_map/pallas_call | solution.py:256
  28.2 1.6 %copy.14 = bf16[80,1,5,128]{3,0,2,1:T(8,128)(2,1)} copy(bf16[80,1,5,128]{3,2,1,0:T(8,128)(2,1)} %shard_map.127) | data formatting | bytes 204800 | tf_op jit(solution)/shard_map/pallas_call | solution.py:256

commit v2 on v1

v2 whole, which is shorter than its diff:
```python
import functools

import jax
import jax.numpy as jnp
from jax import lax
from jax.experimental import pallas as pl
from jax.experimental.pallas import tpu as pltpu
from jax.sharding import PartitionSpec as P

epsilon = 1e-05
MESH = pl.DeviceIdType.MESH
f32 = jnp.float32
bf16 = jnp.bfloat16


def layer_norm(values, gain, bias):
    center = jnp.mean(values, axis=-1, keepdims=True)
    moved = values - center
    spread = jnp.mean(jnp.square(moved), axis=-1, keepdims=True)
    return moved * lax.rsqrt(spread + epsilon) * gain + bias


def sigmoid(values):
    return 0.5 * jnp.tanh(0.5 * values) + 0.5


def chunk_of(total):
    return max(size for size in range(16, 513, 16) if total % size == 0)


def nearest(me, step, count):
    ends = jnp.minimum(me, count - 1 - me)
    between = jnp.where(step % 2 == 1, me + (step + 1) // 2, me - step // 2)
    outside = jnp.where(me <= count - 1 - me, step, count - 1 - step)
    return jnp.where(step <= 2 * ends, between, outside)


def kernel(
    n_row, n_col, group_i, group_j,
    pair_ref, mask_ref, norm_gain, norm_bias, proj_ref, tri_gain, tri_bias,
    trans_gain, trans_bias, gate_hbm, out_w_hbm, trans_in_hbm, trans_out_hbm,
    out_ref,
    flat, work, left_t, right_f, gate, part, own, tri, msg, wide,
    gate_ref, out_w_ref, trans_in, trans_out,
    state_send, state_recv, right_own, left_all, right_all, sum_send, sum_recv, upd_send, upd_recv,
    load_sem, state_sem, l_send, l_recv, r_send, r_recv, b_send, b_recv, c_send, c_recv,
):
    rows, cols, channels = pair_ref.shape
    hidden = proj_ref.shape[1] // 4
    tokens = mask_ref.shape[1]
    total = rows * cols
    piece = cols // n_row
    ratio = cols // rows
    expansion = trans_out.shape[0]
    chunk = chunk_of(total)
    r = lax.axis_index("row")
    q = lax.axis_index("col")
    g, h = r // group_i, r % group_i

    def holder(row_block, col_block):
        first = col_block * ratio
        row = row_block // group_i * group_i + first // group_j
        return row, (row_block % group_i * group_j + first % group_j) // ratio

    tile_row = g * group_i + q * ratio // group_j
    tile_col = (h * group_j + q * ratio % group_j) // ratio

    barrier = pltpu.get_barrier_semaphore()
    devices = n_row * n_col

    @pl.loop(1, devices)
    def _(d):
        place = (r * n_col + q + d) % devices
        pl.semaphore_signal(
            barrier, inc=1, device_id={"row": place // n_col, "col": place % n_col}, device_id_type=MESH)

    loads = [
        pltpu.make_async_copy(source, target, load_sem.at[n])
        for n, (source, target) in enumerate((
            (gate_hbm, gate_ref), (out_w_hbm, out_w_ref), (trans_in_hbm, trans_in), (trans_out_hbm, trans_out)))]
    for load in loads:
        load.start()

    def over_chunks(step):
        if chunk == total:
            step(0)
        else:
            pl.loop(0, total // chunk)(lambda n: step(pl.multiple_of(n * chunk, 16)))

    for i in range(rows):
        flat[i * cols:(i + 1) * cols, :] = pair_ref[i].astype(f32)

    def pair_weight(base):
        spot = lax.broadcasted_iota(jnp.int32, (chunk, tokens), 0).astype(f32) + (
            jnp.asarray(base, jnp.int32).astype(f32))
        token = lax.broadcasted_iota(jnp.int32, (chunk, tokens), 1).astype(f32)
        row_of = jnp.floor((spot + 0.5) * (1.0 / cols))
        col_of = spot - row_of * cols
        first = (token == row_of + (r * rows).astype(f32)).astype(f32)
        second = (token == col_of + (q * cols).astype(f32)).astype(f32)
        picked = ((first + second) * mask_ref[...].astype(f32)).astype(bf16)
        both = jnp.dot(picked, jnp.ones((tokens, hidden), bf16), preferred_element_type=f32)
        return (both > 1.5).astype(f32)

    def project(base):
        at = pl.ds(base, chunk)
        normed = layer_norm(flat[at, :], norm_gain[...], norm_bias[...]).astype(bf16)
        weight = pair_weight(base)
        both = jnp.dot(normed, proj_ref[...], preferred_element_type=f32)
        panel = weight * sigmoid(both[:, 3 * hidden:]) * both[:, 2 * hidden:3 * hidden]
        right_own[at, :] = panel.astype(bf16)
        panel = weight * sigmoid(both[:, hidden:2 * hidden]) * both[:, :hidden]
        left_all[h, at, :] = panel.astype(bf16)
        state_send[at, :] = flat[at, :].astype(bf16)

    over_chunks(project)
    keeps_right = r // group_j == h
    state_row, state_col = holder(r, q)
    keeps_state = jnp.logical_and(state_row == r, state_col == q)
    pl.semaphore_wait(barrier, devices - 1)

    def right_copy(target, source_slot):
        return pltpu.make_async_remote_copy(
            src_ref=right_own, dst_ref=right_all.at[source_slot],
            send_sem=r_send.at[target], recv_sem=r_recv.at[source_slot],
            device_id={"row": target * group_i + r // group_j}, device_id_type=MESH)

    def left_copy(peer, slot):
        return pltpu.make_async_remote_copy(
            src_ref=left_all.at[slot], dst_ref=left_all.at[slot],
            send_sem=l_send.at[peer], recv_sem=l_recv.at[slot],
            device_id={"row": g * group_i + peer}, device_id_type=MESH)

    state_copy = pltpu.make_async_remote_copy(
        src_ref=state_send, dst_ref=state_recv, send_sem=state_sem.at[0], recv_sem=state_sem.at[1],
        device_id={"row": state_row, "col": state_col}, device_id_type=MESH)

    @pl.loop(0, group_j)
    def _(target):
        @pl.when(target * group_i + r // group_j != r)
        def _():
            right_copy(target, r % group_j).start()

    @pl.loop(1, group_i)
    def _(d):
        left_copy((h + d) % group_i, h).start()

    @pl.when(jnp.logical_not(keeps_state))
    def _():
        state_copy.start()

    @pl.when(keeps_state)
    def _():
        state_recv[...] = state_send[...]

    @pl.when(keeps_right)
    def _():
        right_all[r % group_j] = right_own[...]

    def sum_copy(block, peer):
        return pltpu.make_async_remote_copy(
            src_ref=sum_send.at[block], dst_ref=sum_recv.at[q, block % ratio],
            send_sem=b_send.at[block], recv_sem=b_recv.at[q, block % ratio],
            device_id={"col": peer}, device_id_type=MESH)

    chunk_k = next(size for size in (20, 16, 10, 8, 5, 4, 2, 1) if cols % size == 0)

    def triangle(slot, block):
        right_f[...] = right_all[slot].astype(f32)

        @pl.loop(0, rows // piece)
        def _(part_j):
            def steps(base_k, sums):
                sums = list(sums)
                for k in range(chunk_k):
                    mine = left_t[base_k * chunk_k + k]
                    for j in range(piece):
                        place = (part_j * piece + j) * cols + base_k * chunk_k + k
                        sums[j] = sums[j] + mine * right_f[pl.ds(place, 1), :]
                return tuple(sums)
            sums = tuple(jnp.zeros((rows, hidden), f32) for _ in range(piece))
            if chunk_k == cols:
                sums = steps(0, sums)
            else:
                sums = lax.fori_loop(0, cols // chunk_k, steps, sums)
            for j in range(piece):
                part[pl.ds(part_j * piece + j, rows, stride=rows), :] = sums[j]

        owner = block // ratio

        @pl.when(owner == q)
        def _():
            own[block % ratio] = part[...]

        @pl.when(owner != q)
        def _():
            sum_send[block] = part[...].astype(bf16)
            sum_copy(block, owner).start()

    first_right = jnp.clip(r - h * group_j, 0, group_j - 1)

    @pl.loop(0, group_i)
    def _(d):
        left = (h + d) % group_i

        @pl.when(d > 0)
        def _():
            left_copy(left, left).wait_recv()

        work[...] = left_all[left].astype(f32)
        for k in range(cols):
            left_t[k] = work[pl.ds(k, rows, stride=cols), :]

        @pl.loop(0, group_j)
        def _(e):
            slot = (first_right + e) % group_j

            @pl.when(jnp.logical_and(d == 0, h * group_j + slot != r))
            def _():
                right_copy(0, slot).wait_recv()

            triangle(slot, left * group_j + slot)

    loads[0].wait()
    loads[1].wait()

    @pl.when(jnp.logical_not(keeps_state))
    def _():
        state_copy.wait_recv()

    def gates(base):
        at = pl.ds(base, chunk)
        state = state_recv[at, :].astype(f32)
        normed = layer_norm(state, norm_gain[...], norm_bias[...]).astype(bf16)
        gate[at, :] = sigmoid(jnp.dot(normed, gate_ref[...], preferred_element_type=f32))

    over_chunks(gates)

    for half in range(ratio):
        sums = own[half]
        for d in range(1, n_col):
            other = lax.rem(q + d, n_col)
            pltpu.make_async_remote_copy(
                src_ref=sum_send.at[0], dst_ref=sum_recv.at[other, half],
                send_sem=b_send.at[0], recv_sem=b_recv.at[other, half],
                device_id={"col": other}, device_id_type=MESH).wait_recv()
            sums = sums + sum_recv[other, half].astype(f32)
        if ratio == 1:
            tri[...] = sums
        else:
            part[...] = sums
            for i in range(rows):
                tri[i * cols + half * rows:i * cols + (half + 1) * rows, :] = part[i * rows:(i + 1) * rows, :]

    def update(base):
        at = pl.ds(base, chunk)
        normed = layer_norm(tri[at, :], tri_gain[...], tri_bias[...]).astype(bf16)
        branch = jnp.dot(normed, out_w_ref[...], preferred_element_type=f32)
        work[at, :] = state_recv[at, :].astype(f32) + gate[at, :] * branch

    over_chunks(update)

    def upd_copy(slot, place, peer_row, peer_col):
        return pltpu.make_async_remote_copy(
            src_ref=upd_send.at[slot], dst_ref=upd_recv.at[place],
            send_sem=c_send.at[slot], recv_sem=c_recv.at[place],
            device_id={"row": peer_row, "col": peer_col}, device_id_type=MESH)

    def stays(target):
        return jnp.logical_and(target == r, tile_col == q)

    msg[...] = jnp.zeros_like(msg)

    @pl.loop(0, n_row)
    def _(step):
        target = nearest(r, n_row - 1 - step, n_row)
        for j in range(piece):
            msg[j * rows:(j + 1) * rows, :] = work[pl.ds(target * piece + j, rows, stride=cols), :]

        @pl.when(stays(target))
        def _():
            upd_recv[tile_row] = msg[...].astype(bf16)

        @pl.when(jnp.logical_not(stays(target)))
        def _():
            upd_send[target] = msg[...].astype(bf16)
            upd_copy(target, tile_row, target, tile_col).start()

    loads[2].wait()
    loads[3].wait()

    def transition(source):
        state = upd_recv[source].astype(f32)
        normed = layer_norm(state, trans_gain[...], trans_bias[...]).astype(bf16)
        inner = jnp.dot(normed, trans_in[...], preferred_element_type=f32)
        swish = inner[:, :expansion]
        active = (swish * sigmoid(swish) * inner[:, expansion:]).astype(bf16)
        result = state + jnp.dot(active, trans_out[...], preferred_element_type=f32)
        for j in range(piece):
            wide[pl.ds(j, rows, stride=8), :] = result[j * rows:(j + 1) * rows, :]
        out_ref[pl.ds(source * rows, rows), 0] = wide[...].reshape(rows, 8, channels)[:, :piece].astype(bf16)

    wide[...] = jnp.zeros_like(wide)

    @pl.loop(0, n_row)
    def _(step):
        source = nearest(r, step, n_row)
        from_row, from_col = holder(source, q)

        @pl.when(jnp.logical_or(from_row != r, from_col != q))
        def _():
            upd_copy(source, source, from_row, from_col).wait_recv()

        transition(source)

    @pl.loop(0, n_row)
    def _(target):
        @pl.when(jnp.logical_not(stays(target)))
        def _():
            upd_copy(target, tile_row, target, tile_col).wait_send()

        @pl.when(target // ratio != q)
        def _():
            sum_copy(target, target // ratio).wait_send()

    @pl.loop(0, group_j)
    def _(target):
        @pl.when(target * group_i + r // group_j != r)
        def _():
            right_copy(target, r % group_j).wait_send()

    @pl.loop(1, group_i)
    def _(d):
        left_copy((h + d) % group_i, h).wait_send()

    @pl.when(jnp.logical_not(keeps_state))
    def _():
        state_copy.wait_send()


def body(n_row, n_col, pair_state, token_mask, norm_gain, norm_bias, proj_weight, gate_weight,
         tri_gain, tri_bias, out_weight, trans_gain, trans_bias, trans_in, trans_out):
    rows, cols, channels = pair_state.shape
    hidden = proj_weight.shape[1] // 4
    piece = cols // n_row
    ratio = cols // rows
    padded = -(-piece * rows // 16) * 16
    group_i = max(size for size in range(1, n_row + 1) if n_row % size == 0 and size * size <= n_row)
    group_j = n_row // group_i
    flat = lambda count: pltpu.VMEM((count, hidden), f32)
    half = lambda *shape: pltpu.VMEM(shape + (hidden,), bf16)
    line = lambda values: values.reshape(1, -1)
    sems = lambda *shape: pltpu.SemaphoreType.DMA(shape)
    return pl.pallas_call(
        functools.partial(kernel, n_row, n_col, group_i, group_j),
        out_shape=jax.ShapeDtypeStruct((rows * n_row, 1, piece, channels), bf16),
        in_specs=[pl.BlockSpec(memory_space=pltpu.VMEM)] * 9 + [pl.BlockSpec(memory_space=pl.ANY)] * 4,
        out_specs=pl.BlockSpec(memory_space=pltpu.VMEM),
        scratch_shapes=[
            flat(rows * cols), flat(rows * cols),
            pltpu.VMEM((cols, rows, hidden), f32),
            flat(rows * cols), flat(rows * cols), flat(rows * rows),
            pltpu.VMEM((ratio, rows * rows, hidden), f32),
            flat(rows * cols), flat(padded), flat(rows * 8),
            pltpu.VMEM(gate_weight.shape, bf16), pltpu.VMEM(out_weight.shape, bf16),
            pltpu.VMEM(trans_in.shape, bf16), pltpu.VMEM(trans_out.shape, bf16),
            half(rows * cols), half(rows * cols), half(rows * cols),
            half(group_i, rows * cols), half(group_j, rows * cols),
            half(n_row, rows * rows), half(n_col, ratio, rows * rows),
            half(n_row, padded), half(n_row, padded),
            sems(4), sems(2), sems(group_i), sems(group_i), sems(group_j), sems(group_j),
            sems(n_row), sems(n_col, ratio), sems(n_row), sems(n_row),
        ],
        compiler_params=pltpu.CompilerParams(
            collective_id=0, has_side_effects=True, vmem_limit_bytes=56 * 1024 * 1024),
    )(pair_state, line(token_mask), line(norm_gain), line(norm_bias), proj_weight,
      line(tri_gain), line(tri_bias), line(trans_gain), line(trans_bias),
      gate_weight, out_weight, trans_in, trans_out)


def solution(mesh):
    in_specs = (P(("groups", "row"), "col", None), P("groups")) + (P(),) * 11
    out_specs = P("groups", "col", "row", None)
    return jax.shard_map(
        functools.partial(body, mesh.shape["row"], mesh.shape["col"]),
        mesh=mesh, in_specs=in_specs, out_specs=out_specs, check_vma=False)
```

time: 29.9 us -> 27.7 us (0.926)
  Pallas kernels: 28.2 us -> 26 us
    pallas_call x1, Pallas kernels: 28.2 us -> 26 us  [body(): pl.pallas_call(functools.partial(kernel, n_row, n_col, group_i, group_j),...]
where the time goes in v2:
time: 27.7 us; the launch traced here: 27.5 us
  Pallas kernels  26 us (94%)
  local copies, waits for them, and re-layouts  1.57 us (6%)
    pallas_call x1, Pallas kernels, body(): pl.pallas_call(functools.partial(kernel, n_row, n_col, group_i, group_j),...  26 us
    pallas_call x1, local copies, waits for them, and re-layouts, body(): pl.pallas_call(functools.partial(kernel, n_row, n_col, group_i, group_j),...  1.57 us

profile of v2, /device:TPU:0, one launch (start us, length us, event | category | flops | bytes accessed | tf_op | source)
XLA Modules:
  0.0 27.5 jit_solution(3814230656943920453)
XLA Ops:
  0.0 26.0 %shard_map.127 = bf16[80,1,5,128]{3,2,1,0:T(8,128)(2,1)} custom-call(bf16[20,20,128]{2,1,0:T(8,128)(2,1)} %pair_ref.1, s32[1,80]{1,0:T(1,128)} %bitcast.7, f32[1,128]{1,0:T(1,128)} %bitcast.8, f32[1,128]{1,0:T(1,128)} %bitcast.9, bf16[128,512]{1,0:T(8,128)(2,1)} %proj_ref.1, f32[1,128]{1,0:T(1,128)} %bitcast.10, f32[1,128]{1,0:T(1,128)} %bitcast.11, ...), custom_call_target="tpu_custom_call" | custom-call | tf_op jit(solution)/shard_map/pallas_call | solution.py:354
  26.0 1.6 %copy.14 = bf16[80,1,5,128]{3,0,2,1:T(8,128)(2,1)} copy(bf16[80,1,5,128]{3,2,1,0:T(8,128)(2,1)} %shard_map.127) | data formatting | bytes 204800 | tf_op jit(solution)/shard_map/pallas_call | solution.py:354

commit v3 on v2

--- a/solution.py
+++ b/solution.py
@@ -135,15 +135,15 @@
         src_ref=state_send, dst_ref=state_recv, send_sem=state_sem.at[0], recv_sem=state_sem.at[1],
         device_id={"row": state_row, "col": state_col}, device_id_type=MESH)
 
+    @pl.loop(1, group_i)
+    def _(d):
+        left_copy((h + d) % group_i, h).start()
+
     @pl.loop(0, group_j)
     def _(target):
         @pl.when(target * group_i + r // group_j != r)
         def _():
             right_copy(target, r % group_j).start()
-
-    @pl.loop(1, group_i)
-    def _(d):
-        left_copy((h + d) % group_i, h).start()
 
     @pl.when(jnp.logical_not(keeps_state))
     def _():
@@ -165,15 +165,13 @@
 
     chunk_k = next(size for size in (20, 16, 10, 8, 5, 4, 2, 1) if cols % size == 0)
 
-    def triangle(slot, block):
-        right_f[...] = right_all[slot].astype(f32)
-
+    def triangle(left, block):
         @pl.loop(0, rows // piece)
         def _(part_j):
             def steps(base_k, sums):
                 sums = list(sums)
                 for k in range(chunk_k):
-                    mine = left_t[base_k * chunk_k + k]
+                    mine = left_t[left, base_k * chunk_k + k]
                     for j in range(piece):
                         place = (part_j * piece + j) * cols + base_k * chunk_k + k
                         sums[j] = sums[j] + mine * right_f[pl.ds(place, 1), :]
@@ -199,27 +197,31 @@
 
     first_right = jnp.clip(r - h * group_j, 0, group_j - 1)
 
-    @pl.loop(0, group_i)
-    def _(d):
-        left = (h + d) % group_i
-
-        @pl.when(d > 0)
-        def _():
-            left_copy(left, left).wait_recv()
-
-        work[...] = left_all[left].astype(f32)
-        for k in range(cols):
-            left_t[k] = work[pl.ds(k, rows, stride=cols), :]
-
-        @pl.loop(0, group_j)
-        def _(e):
-            slot = (first_right + e) % group_j
-
-            @pl.when(jnp.logical_and(d == 0, h * group_j + slot != r))
+    @pl.loop(0, group_j)
+    def _(e):
+        slot = (first_right + e) % group_j
+
+        @pl.when(h * group_j + slot != r)
+        def _():
+            right_copy(0, slot).wait_recv()
+
+        right_f[...] = right_all[slot].astype(f32)
+
+        @pl.loop(0, group_i)
+        def _(d):
+            left = jnp.where(e == 0, h + d, q * group_i // n_col + 1 + d) % group_i
+
+            @pl.when(jnp.logical_and(e == 0, d > 0))
             def _():
-                right_copy(0, slot).wait_recv()
-
-            triangle(slot, left * group_j + slot)
+                left_copy(left, left).wait_recv()
+
+            @pl.when(e == 0)
+            def _():
+                work[...] = left_all[left].astype(f32)
+                for k in range(cols):
+                    left_t[left, k] = work[pl.ds(k, rows, stride=cols), :]
+
+            triangle(left, left * group_j + slot)
 
     loads[0].wait()
     loads[1].wait()
@@ -358,7 +360,7 @@
         out_specs=pl.BlockSpec(memory_space=pltpu.VMEM),
         scratch_shapes=[
             flat(rows * cols), flat(rows * cols),
-            pltpu.VMEM((cols, rows, hidden), f32),
+            pltpu.VMEM((group_i, cols, rows, hidden), f32),
             flat(rows * cols), flat(rows * cols), flat(rows * rows),
             pltpu.VMEM((ratio, rows * rows, hidden), f32),
             flat(rows * cols), flat(padded), flat(rows * 8),

time: 27.7 us -> 26.6 us (0.960)
  Pallas kernels: 26 us -> 24.9 us
    pallas_call x1, Pallas kernels: 26 us -> 24.9 us  [body(): pl.pallas_call(functools.partial(kernel, n_row, n_col, group_i, group_j),...]
where the time goes in v3:
time: 26.6 us; the launch traced here: 26.5 us
  Pallas kernels  24.9 us (94%)
  local copies, waits for them, and re-layouts  1.57 us (6%)
    pallas_call x1, Pallas kernels, body(): pl.pallas_call(functools.partial(kernel, n_row, n_col, group_i, group_j),...  24.9 us
    pallas_call x1, local copies, waits for them, and re-layouts, body(): pl.pallas_call(functools.partial(kernel, n_row, n_col, group_i, group_j),...  1.57 us

profile of v3, /device:TPU:0, one launch (start us, length us, event | category | flops | bytes accessed | tf_op | source)
XLA Modules:
  0.0 26.5 jit_solution(4930980251150710400)
XLA Ops:
  0.0 24.9 %shard_map.127 = bf16[80,1,5,128]{3,2,1,0:T(8,128)(2,1)} custom-call(bf16[20,20,128]{2,1,0:T(8,128)(2,1)} %pair_ref.1, s32[1,80]{1,0:T(1,128)} %bitcast.7, f32[1,128]{1,0:T(1,128)} %bitcast.8, f32[1,128]{1,0:T(1,128)} %bitcast.9, bf16[128,512]{1,0:T(8,128)(2,1)} %proj_ref.1, f32[1,128]{1,0:T(1,128)} %bitcast.10, f32[1,128]{1,0:T(1,128)} %bitcast.11, ...), custom_call_target="tpu_custom_call" | custom-call | tf_op jit(solution)/shard_map/pallas_call | solution.py:356
  24.9 1.6 %copy.14 = bf16[80,1,5,128]{3,0,2,1:T(8,128)(2,1)} copy(bf16[80,1,5,128]{3,2,1,0:T(8,128)(2,1)} %shard_map.127) | data formatting | bytes 204800 | tf_op jit(solution)/shard_map/pallas_call | solution.py:356
